TPU v7x, 256 devices: a whole 4x4x8 slice. The times are simulated.
256 devices in a mesh: dec: 32 (over y, x, core), ch: 8 (over z).
Axes of the slice: x: 4, y: 4, z: 8, core: 2. Of those that a mesh axis runs over, the one named last changes fastest.
Arguments:
- frame_cotangent: bfloat16 [256, 160, 8192], P('dec', None, 'ch'), may hold values from -5 to 5
- rollout_utterance: int32 [256], P('dec'), may hold values from 0 to 31, as said below
- frame_offset: int32 [256], P('dec'), may hold values from 0 to 32
- utterance_frames: int32 [32], P('dec'), may hold values from 1 to 128, 3072 in all
- normed_input: bfloat16 [32, 128, 1024], P('dec', None, 'ch'), may hold values from -6 to 6
- expand_weight: bfloat16 [1024, 2, 1024], P(None, None, 'ch'), may hold values from -0.1875 to 0.1875
- depth_kernel: bfloat16 [9, 1024], P(None, 'ch'), may hold values from -2 to 2
- norm_scale: float32 [1024], P('ch'), may hold values from 0.1 to 1.9
- norm_shift: float32 [1024], P('ch'), may hold values from -3 to 3
- project_weight: bfloat16 [1024, 1024], replicated, may hold values from -0.1875 to 0.1875
- adapter_weight: bfloat16 [1024, 8192], P(None, 'ch'), may hold values from -0.0625 to 0.0625
Outputs:
- grad_stream: bfloat16 [32, 128, 1024], P('dec', None, 'ch')
- grad_normed: bfloat16 [32, 128, 1024], P('dec', None, 'ch')
Inputs may be any that keep to these rules, and one draw needn't show every extreme that they name: `rollout_utterance`: each utterance is named by exactly 8 rollouts; utterances k * 1 to (k + 1) - 1 are owned by index k of dec; among the 8 rollouts of one index of dec at most 1 name utterances of one owner, and some owner is named exactly 1 times; the rollouts of index k of dec always name some utterance of the owner (k + 16) mod 32.
All inputs are finite; a program needn't handle non-finite values. No bound on the sum of `utterance_frames` on one device may be relied on, other than what follows from the above.
Results may differ from a plain program's by a relative error of at most 0.03.
Values may be sent and summed in bfloat16 or wider, within the bound.
A program may use at most 128 MiB of HBM per device.

v0:
```python
import jax
import jax.numpy as jnp
from jax import lax
from jax.sharding import PartitionSpec as P


def body(
    frame_cotangent,
    rollout_utterance,
    frame_offset,
    utterance_frames,
    normed_input,
    expand_weight,
    depth_kernel,
    norm_scale,
    norm_shift,
    project_weight,
    adapter_weight,
):
    local_rolls, seq_len, d_local = frame_cotangent.shape
    u_local, frames, c_local = normed_input.shape
    width = expand_weight.shape[0]
    taps = depth_kernel.shape[0]
    row_count = u_local * frames
    slabs = jax.vmap(lambda window, first: lax.dynamic_slice_in_dim(window, first, frames, 0))(
        frame_cotangent, frame_offset
    )
    flat_slabs = slabs.reshape(local_rolls, frames * d_local)
    target = jnp.arange(lax.axis_size("dec") * u_local, dtype=jnp.int32)
    select = (target[:, None] == rollout_utterance[None, :]).astype(jnp.bfloat16)
    rounded = lax.optimization_barrier(
        jnp.dot(select, flat_slabs, preferred_element_type=jnp.float32).astype(jnp.bfloat16)
    )
    received = lax.psum_scatter(
        rounded.astype(jnp.float32).astype(jnp.bfloat16), "dec", scatter_dimension=0, tiled=True
    ).astype(jnp.float32)
    frame_index = jnp.arange(frames, dtype=jnp.int32)
    mask = (frame_index[None, :] < utterance_frames[:, None]).astype(jnp.float32)
    frame_grad = (received.reshape(u_local, frames, d_local) * mask[:, :, None]).astype(
        jnp.bfloat16
    )
    grad_rows = frame_grad.reshape(row_count, d_local)
    block = adapter_weight
    stream_cols = lax.psum_scatter(
        lax.dot_general(
            block, grad_rows, (((1,), (1,)), ((), ())), preferred_element_type=jnp.float32
        ).astype(jnp.bfloat16),
        "ch",
        scatter_dimension=0,
        tiled=True,
    ).astype(jnp.float32)
    grad_stream = stream_cols.T.astype(jnp.bfloat16)
    expand_flat = expand_weight.reshape(width, 2 * c_local)
    piece = lax.all_gather(normed_input, "ch", axis=2, tiled=True)
    span = piece.shape[2]
    block = expand_flat
    expanded = jnp.dot(piece.reshape(row_count, span), block, preferred_element_type=jnp.float32)
    value = expanded[:, :c_local]
    gate = expanded[:, c_local:]
    sig_gate = jax.nn.sigmoid(gate)
    mask_rows = mask.reshape(row_count, 1)
    glu = (mask_rows * value * sig_gate).reshape(u_local, frames, c_local)
    kernel = depth_kernel.astype(jnp.float32)
    half = (taps - 1) // 2
    padded = jnp.pad(glu, ((0, 0), (half, half), (0, 0)))
    depth = jnp.zeros((u_local, frames, c_local), jnp.float32)
    for step in range(taps):
        depth = depth + kernel[step] * padded[:, step : step + frames, :]
    shifted = depth * norm_scale + norm_shift
    ch_start = lax.axis_index("ch") * c_local
    own_rows = lax.dynamic_slice_in_dim(project_weight, ch_start, c_local, 0)
    grad_swish = lax.dot_general(
        lax.all_gather(grad_stream, "ch", axis=1, tiled=True),
        own_rows,
        (((1,), (1,)), ((), ())),
        preferred_element_type=jnp.float32,
    )
    grad_swish = grad_swish.reshape(u_local, frames, c_local)
    sig_shift = jax.nn.sigmoid(shifted)
    grad_depth = grad_swish * sig_shift * (1.0 + shifted * (1.0 - sig_shift)) * norm_scale
    padded_back = jnp.pad(grad_depth, ((0, 0), (half, half), (0, 0)))
    grad_glu = jnp.zeros((u_local, frames, c_local), jnp.float32)
    for step in range(taps):
        grad_glu = (
            grad_glu + kernel[step] * padded_back[:, taps - 1 - step : taps - 1 - step + frames, :]
        )
    grad_glu = grad_glu.reshape(row_count, c_local) * mask_rows
    grad_value = grad_glu * sig_gate
    grad_gate = grad_glu * value * sig_gate * (1.0 - sig_gate)
    grad_expanded = jnp.concatenate([grad_value, grad_gate], axis=1).astype(jnp.bfloat16)
    block = expand_flat
    input_cols = lax.psum_scatter(
        lax.dot_general(
            block, grad_expanded, (((1,), (1,)), ((), ())), preferred_element_type=jnp.float32
        ).astype(jnp.bfloat16),
        "ch",
        scatter_dimension=0,
        tiled=True,
    ).astype(jnp.float32)
    grad_normed = input_cols.T.astype(jnp.bfloat16)
    return (
        grad_stream.reshape(u_local, frames, c_local),
        grad_normed.reshape(u_local, frames, c_local),
    )


def solution(mesh):
    return jax.shard_map(
        body,
        mesh=mesh,
        in_specs=(
            P("dec", None, "ch"),
            P("dec"),
            P("dec"),
            P("dec"),
            P("dec", None, "ch"),
            P(None, None, "ch"),
            P(None, "ch"),
            P("ch"),
            P("ch"),
            P(),
            P(None, "ch"),
        ),
        out_specs=(P("dec", None, "ch"), P("dec", None, "ch")),
        check_vma=False,
    )
```

profile of v0, /device:TPU:2, one launch (start us, length us, event | category | flops | bytes accessed | tf_op | source)
XLA Modules:
  0.0 291.1 jit_solution(7985115832883132730)
XLA Ops:
  7.2 0.0 copy-start
  7.2 0.0 all-reduce.6.cloned.1.call-start
  7.2 0.8 fusion.34
  8.0 29.7 %while.1 = (s32[]{:T(128)}, bf16[8,160,1024]{2,1,0:T(8,128)(2,1)}, s32[8,3]{0,1:T(4,128)S(1)}, bf16[8,128,1024]{2,1,0:T(8,128)(2,1)}, s32[]{:T(128)}) while((s32[]{:T(128)}, bf16[8,160,1024]{2,1,0:T(8,128)(2,1)}, s32[8,3]{0,1:T(4,128)S(1)}, bf16[8,128,1024]{2,1,0:T(8,128)(2,1)}, s32[]{:T(128)}) %tuple.32), condition=%wide.while_cond, body=%wide.while_body.sunk | while | flops 2 | bytes 525429 | solution.py:25
  8.1 0.1 constant_dynamic-slice_fusion.2
  8.1 0.6 fusion.42
  8.7 3.1 %dynamic-slice_dynamic-update-slice_fusion.2 = bf16[8,128,1024]{2,1,0:T(8,128)(2,1)} fusion(bf16[8,128,1024]{2,1,0:T(8,128)(2,1)} %get-tuple-element.68, s32[]{:T(128)S(6)} %copy.30, bf16[8,160,1024]{2,1,0:T(8,128)(2,1)} %get-tuple-element.71, s32[]{:T(128)} %bitcast.81, s32[]{:T(128)} %bitcast.82), kind=kLoop, calls=%fused_computation.clone.1 | loop fusion | bytes 525316 | tf_op jit(solution)/shard_map/vmap()/gather
  11.8 0.1 constant_dynamic-slice_fusion.2
  11.8 0.6 fusion.42
  12.4 3.1 %dynamic-slice_dynamic-update-slice_fusion.2 = bf16[8,128,1024]{2,1,0:T(8,128)(2,1)} fusion(bf16[8,128,1024]{2,1,0:T(8,128)(2,1)} %get-tuple-element.68, s32[]{:T(128)S(6)} %copy.30, bf16[8,160,1024]{2,1,0:T(8,128)(2,1)} %get-tuple-element.71, s32[]{:T(128)} %bitcast.81, s32[]{:T(128)} %bitcast.82), kind=kLoop, calls=%fused_computation.clone.1 | loop fusion | bytes 525316 | tf_op jit(solution)/shard_map/vmap()/gather
  15.5 0.1 constant_dynamic-slice_fusion.2
  15.6 0.6 fusion.42
  16.1 3.0 %dynamic-slice_dynamic-update-slice_fusion.2 = bf16[8,128,1024]{2,1,0:T(8,128)(2,1)} fusion(bf16[8,128,1024]{2,1,0:T(8,128)(2,1)} %get-tuple-element.68, s32[]{:T(128)S(6)} %copy.30, bf16[8,160,1024]{2,1,0:T(8,128)(2,1)} %get-tuple-element.71, s32[]{:T(128)} %bitcast.81, s32[]{:T(128)} %bitcast.82), kind=kLoop, calls=%fused_computation.clone.1 | loop fusion | bytes 525316 | tf_op jit(solution)/shard_map/vmap()/gather
  19.2 0.1 constant_dynamic-slice_fusion.2
  19.3 0.6 fusion.42
  19.8 3.0 %dynamic-slice_dynamic-update-slice_fusion.2 = bf16[8,128,1024]{2,1,0:T(8,128)(2,1)} fusion(bf16[8,128,1024]{2,1,0:T(8,128)(2,1)} %get-tuple-element.68, s32[]{:T(128)S(6)} %copy.30, bf16[8,160,1024]{2,1,0:T(8,128)(2,1)} %get-tuple-element.71, s32[]{:T(128)} %bitcast.81, s32[]{:T(128)} %bitcast.82), kind=kLoop, calls=%fused_computation.clone.1 | loop fusion | bytes 525316 | tf_op jit(solution)/shard_map/vmap()/gather
  22.9 0.1 constant_dynamic-slice_fusion.2
  22.9 0.6 fusion.42
  23.5 3.1 %dynamic-slice_dynamic-update-slice_fusion.2 = bf16[8,128,1024]{2,1,0:T(8,128)(2,1)} fusion(bf16[8,128,1024]{2,1,0:T(8,128)(2,1)} %get-tuple-element.68, s32[]{:T(128)S(6)} %copy.30, bf16[8,160,1024]{2,1,0:T(8,128)(2,1)} %get-tuple-element.71, s32[]{:T(128)} %bitcast.81, s32[]{:T(128)} %bitcast.82), kind=kLoop, calls=%fused_computation.clone.1 | loop fusion | bytes 525316 | tf_op jit(solution)/shard_map/vmap()/gather
  26.6 0.1 constant_dynamic-slice_fusion.2
  26.7 0.6 fusion.42
  27.2 3.1 %dynamic-slice_dynamic-update-slice_fusion.2 = bf16[8,128,1024]{2,1,0:T(8,128)(2,1)} fusion(bf16[8,128,1024]{2,1,0:T(8,128)(2,1)} %get-tuple-element.68, s32[]{:T(128)S(6)} %copy.30, bf16[8,160,1024]{2,1,0:T(8,128)(2,1)} %get-tuple-element.71, s32[]{:T(128)} %bitcast.81, s32[]{:T(128)} %bitcast.82), kind=kLoop, calls=%fused_computation.clone.1 | loop fusion | bytes 525316 | tf_op jit(solution)/shard_map/vmap()/gather
  30.3 0.1 constant_dynamic-slice_fusion.2
  30.4 0.6 fusion.42
  31.0 3.1 %dynamic-slice_dynamic-update-slice_fusion.2 = bf16[8,128,1024]{2,1,0:T(8,128)(2,1)} fusion(bf16[8,128,1024]{2,1,0:T(8,128)(2,1)} %get-tuple-element.68, s32[]{:T(128)S(6)} %copy.30, bf16[8,160,1024]{2,1,0:T(8,128)(2,1)} %get-tuple-element.71, s32[]{:T(128)} %bitcast.81, s32[]{:T(128)} %bitcast.82), kind=kLoop, calls=%fused_computation.clone.1 | loop fusion | bytes 525316 | tf_op jit(solution)/shard_map/vmap()/gather
  34.0 0.1 constant_dynamic-slice_fusion.2
  34.1 0.6 fusion.42
  34.7 3.1 %dynamic-slice_dynamic-update-slice_fusion.2 = bf16[8,128,1024]{2,1,0:T(8,128)(2,1)} fusion(bf16[8,128,1024]{2,1,0:T(8,128)(2,1)} %get-tuple-element.68, s32[]{:T(128)S(6)} %copy.30, bf16[8,160,1024]{2,1,0:T(8,128)(2,1)} %get-tuple-element.71, s32[]{:T(128)} %bitcast.81, s32[]{:T(128)} %bitcast.82), kind=kLoop, calls=%fused_computation.clone.1 | loop fusion | bytes 525316 | tf_op jit(solution)/shard_map/vmap()/gather
  37.7 2.8 copy.17
  40.5 0.0 copy-done.5
  40.5 5.5 %convolution_convert_fusion = bf16[32,131072]{1,0:T(8,128)(2,1)} fusion(bf16[8,131072]{1,0:T(8,128)(2,1)S(1)} %bitcast.84, s32[8]{0:T(128)S(1)} %copy-done.5), kind=kOutput, calls=%fused_computation.2 | convolution fusion | flops 71303424 | bytes 10485792 | tf_op jit(solution)/shard_map/dot_general | solution.py:32
  46.1 0.0 all-reduce.6.cloned.1.call-update
  46.1 0.0 reduce-scatter.7.cloned.1.call-start
  46.8 0.0 copy-done.4
  46.8 0.0 copy-done.8
  46.8 0.6 dynamic-slice.4
  47.4 132.1 %all-reduce.6.cloned.1.call-done = bf16[32,131072]{1,0:T(8,128)(2,1)} async-done(((bf16[32,131072]{1,0:T(8,128)(2,1)}), bf16[32,131072]{1,0:T(8,128)(2,1)}) %all-reduce.6.cloned.1.call-update) | async-done | bytes 8388624
  179.5 3.8 %fusion.8 = f32[131072]{0:T(1024)S(1)} fusion(bf16[32,131072]{1,0:T(8,128)(2,1)} %all-reduce.6.cloned.1.call-done, u32[]{:T(128)} %bitcast.26), kind=kLoop, calls=%fused_computation.15 | loop fusion | flops 131072 | bytes 786436 | tf_op jit(solution)/shard_map/reshape | solution.py:39
  183.3 0.1 reshape.134
  183.4 0.0 copy-done
  183.4 0.0 copy-start.3
  183.5 0.0 copy-start.1
  183.5 0.0 copy-start.6
  183.5 0.0 copy-start.7
  183.5 0.8 fusion
  184.3 0.9 copy.13
  185.2 0.0 reduce-scatter.7.cloned.1.call-update
  185.2 0.0 reduce-scatter.9.cloned.1.call-start
  185.3 0.0 copy-done.3
  185.3 24.9 %all_gather.7 = bf16[1,128,1024]{2,1,0:T(8,128)(2,1)S(1)} all-gather(bf16[1,128,128]{2,1,0:T(8,128)(2,1)S(1)} %copy-done.3), channel_id=1, replica_groups=mesh['dec'=32,'ch'=8] {'ch'}, dimensions={2}, use_global_device_ids=true | all-gather | bytes 294912 | tf_op jit(solution)/shard_map/all_gather | solution.py:54
  210.2 0.2 fusion.6
  210.4 0.1 fusion.33
  210.5 11.6 %reduce-scatter.7.cloned.1.call-done = bf16[128,128]{1,0:T(8,128)(2,1)} async-done(((bf16[1024,128]{1,0:T(8,128)(2,1)}), bf16[128,128]{1,0:T(8,128)(2,1)}) %reduce-scatter.7.cloned.1.call-update) | async-done | bytes 32784
  222.1 0.9 copy.14
  223.0 0.0 copy-start.2
  223.0 22.2 %all_gather.6 = bf16[128,1024]{1,0:T(8,128)(2,1)S(1)} all-gather(bf16[128,128]{1,0:T(8,128)(2,1)S(1)} %bitcast.88), channel_id=1, replica_groups=mesh['dec'=32,'ch'=8] {'ch'}, dimensions={1}, use_global_device_ids=true | all-gather | bytes 294912 | tf_op jit(solution)/shard_map/all_gather | solution.py:73
  245.2 0.0 copy-done.7
  245.2 1.2 fusion.4
  246.4 0.1 multiply_convert_fusion.3
  246.5 0.3 fusion.1
  246.8 0.9 copy.15
  247.7 0.0 reduce-scatter.9.cloned.1.call-update
  247.7 35.4 %reduce-scatter.9.cloned.1.call-done = bf16[128,128]{1,0:T(8,128)(2,1)} async-done(((bf16[1024,128]{1,0:T(8,128)(2,1)}), bf16[128,128]{1,0:T(8,128)(2,1)}) %reduce-scatter.9.cloned.1.call-update) | async-done | bytes 32784
  283.1 1.5 copy.16
  (13 shorter events, 0.1 us)
Async XLA Ops:
  7.2 176.3 %copy-start = (bf16[1024,1024]{1,0:T(8,128)(2,1)S(1)}, bf16[1024,1024]{1,0:T(8,128)(2,1)}, u32[]{:S(2)}) copy-start(bf16[1024,1024]{1,0:T(8,128)(2,1)} %param.21) | copy-start | bytes 6291460
  7.2 172.3 %all-reduce.6.cloned.1.call-start = ((), (), s32[]{:S(2)}) async-start(), calls=%async_computation.4 | async-start | bytes 16777216
  37.7 2.8 copy-start.5
  46.0 0.7 copy-start.4
  46.1 0.8 copy-start.8
  46.1 176.0 %reduce-scatter.7.cloned.1.call-start = ((), (), s32[]{:S(2)}) async-start(), calls=%async_computation.2 | async-start | bytes 294912
  183.4 1.8 copy-start.3
  183.5 26.7 %copy-start.1 = (bf16[1024,2,128]{2,1,0:T(2,128)(2,1)S(1)}, bf16[1024,2,128]{2,1,0:T(2,128)(2,1)}, u32[]{:S(2)}) copy-start(bf16[1024,2,128]{2,1,0:T(2,128)(2,1)} %param.16) | copy-start | bytes 1572868
  183.5 61.7 %copy-start.6 = (f32[128]{0:T(128)S(1)}, f32[128]{0:T(128)}, u32[]{:S(2)}) copy-start(f32[128]{0:T(128)} %param.19) | copy-start | bytes 1540
  183.5 61.7 %copy-start.7 = (f32[128]{0:T(128)S(1)}, f32[128]{0:T(128)}, u32[]{:S(2)}) copy-start(f32[128]{0:T(128)} %param.18) | copy-start | bytes 1540
  185.2 97.9 %reduce-scatter.9.cloned.1.call-start = ((), (), s32[]{:S(2)}) async-start(), calls=%async_computation.3 | async-start | bytes 294912
  223.0 61.6 %copy-start.2 = (bf16[128,128]{0,1:T(8,128)(2,1)}, bf16[128,128]{0,1:T(8,128)(2,1)S(1)}, u32[]{:S(2)}) copy-start(bf16[128,128]{0,1:T(8,128)(2,1)S(1)} %copy.14) | copy-start | bytes 98308
Sparse Core Ops, SparseCore 0:
  46.2 133.2 all-reduce.5
  185.3 36.7 reduce-scatter.6
  247.8 35.2 reduce-scatter.8
where the time goes:
time: 292 us; the launch traced here: 291 us
  waiting for transfers between devices  179 us (61%)
  blocking collectives  47.1 us (16%)
  local copies, waits for them, and re-layouts  37.2 us (13%)
  between operations  14.6 us (5%)
  matrix products  8.12 us (3%)
  other arithmetic  4.86 us (2%)
    unnamed x6, waiting for transfers between devices  179 us
    gather x24, local copies, waits for them, and re-layouts  29.7 us
    all_gather x1, blocking collectives, body(): piece = lax.all_gather(normed_input, 'ch', axis=2, tiled=True)  24.9 us
    all_gather x1, blocking collectives, body(): lax.all_gather(grad_stream, 'ch', axis=1, tiled=True)  22.2 us
    unnamed x25, local copies, waits for them, and re-layouts  7.43 us
  transfers between devices with their start and end apart: 3, of which 3 were waited for; matrix products, arithmetic and copies ran while one was open for 0% of the time, Pallas kernels for 0%

commit v1 on v0

--- a/solution.py
+++ b/solution.py
@@ -2,6 +2,11 @@
 import jax.numpy as jnp
 from jax import lax
 from jax.sharding import PartitionSpec as P
+
+
+def swapped_in(shard, name, along):
+    stack = jnp.stack([shard] * lax.axis_size(name))
+    return jnp.concatenate(lax.all_to_all(stack, name, 0, 0), axis=along)
 
 
 def body(
@@ -70,7 +75,7 @@
     ch_start = lax.axis_index("ch") * c_local
     own_rows = lax.dynamic_slice_in_dim(project_weight, ch_start, c_local, 0)
     grad_swish = lax.dot_general(
-        lax.all_gather(grad_stream, "ch", axis=1, tiled=True),
+        swapped_in(grad_stream, "ch", 1),
         own_rows,
         (((1,), (1,)), ((), ())),
         preferred_element_type=jnp.float32,

time: 292 us -> 281 us (0.962)
  blocking collectives: 47.1 us -> 24.8 us
  waiting for transfers between devices: 179 us -> 187 us
  starting transfers between devices: 0.12 us -> 4.55 us
    all_gather x1 -> x0, blocking collectives: 22.2 us -> none  [body(): lax.all_gather(grad_stream, 'ch', axis=1, tiled=True)]
    all_to_all x0 -> x1, waiting for transfers between devices: none -> 10 us  [swapped_in(): return jnp.concatenate(lax.all_to_all(stack, name, 0, 0), axis=along)]
    all_to_all x0 -> x1, starting transfers between devices: none -> 4.43 us  [swapped_in(): return jnp.concatenate(lax.all_to_all(stack, name, 0, 0), axis=along)]
  transfers between devices with their start and end apart: 3 -> 4, of which waited for: 3 -> 4; matrix products, arithmetic and copies ran while one was open for 0% -> 1% of each run, Pallas kernels for 0% -> 0%
where the time goes in v1:
time: 281 us
  waiting for transfers between devices  187 us (67%)
  local copies, waits for them, and re-layouts  37.1 us (13%)
  blocking collectives  24.8 us (9%)
  between operations  14.6 us (5%)
  matrix products  8.14 us (3%)
  other arithmetic  4.86 us (2%)
  starting transfers between devices  4.55 us (2%)
    unnamed x6, waiting for transfers between devices  177 us
    gather x24, local copies, waits for them, and re-layouts  28.2 us
    all_gather x1, blocking collectives, body(): piece = lax.all_gather(normed_input, 'ch', axis=2, tiled=True)  24.8 us
    all_to_all x1, waiting for transfers between devices, swapped_in(): return jnp.concatenate(lax.all_to_all(stack, name, 0, 0), axis=along)  10 us
    unnamed x25, local copies, waits for them, and re-layouts  7.28 us
  transfers between devices with their start and end apart: 4, of which 4 were waited for; matrix products, arithmetic and copies ran while one was open for 1% of the time, Pallas kernels for 0%

profile of v1, /device:TPU:2, one launch (start us, length us, event | category | flops | bytes accessed | tf_op | source)
XLA Modules:
  0.0 280.6 jit_solution(7788294665481093370)
XLA Ops:
  7.2 0.0 copy-start
  7.2 0.0 all-reduce.6.cloned.1.call-start
  7.2 0.8 fusion.34
  8.0 28.3 %while.1 = (s32[]{:T(128)}, bf16[8,160,1024]{2,1,0:T(8,128)(2,1)}, s32[8,3]{0,1:T(4,128)S(1)}, bf16[8,128,1024]{2,1,0:T(8,128)(2,1)}, s32[]{:T(128)}) while((s32[]{:T(128)}, bf16[8,160,1024]{2,1,0:T(8,128)(2,1)}, s32[8,3]{0,1:T(4,128)S(1)}, bf16[8,128,1024]{2,1,0:T(8,128)(2,1)}, s32[]{:T(128)}) %tuple.32), condition=%wide.while_cond, body=%wide.while_body.sunk | while | flops 2 | bytes 525429 | solution.py:30
  8.1 0.1 constant_dynamic-slice_fusion.2
  8.1 0.5 fusion.42
  8.7 2.9 %dynamic-slice_dynamic-update-slice_fusion.2 = bf16[8,128,1024]{2,1,0:T(8,128)(2,1)} fusion(bf16[8,128,1024]{2,1,0:T(8,128)(2,1)} %get-tuple-element.68, s32[]{:T(128)S(6)} %copy.33, bf16[8,160,1024]{2,1,0:T(8,128)(2,1)} %get-tuple-element.71, s32[]{:T(128)} %bitcast.85, s32[]{:T(128)} %bitcast.86), kind=kLoop, calls=%fused_computation.clone.1 | loop fusion | bytes 525316 | tf_op jit(solution)/shard_map/vmap()/gather
  11.6 0.1 constant_dynamic-slice_fusion.2
  11.7 0.5 fusion.42
  12.2 2.9 %dynamic-slice_dynamic-update-slice_fusion.2 = bf16[8,128,1024]{2,1,0:T(8,128)(2,1)} fusion(bf16[8,128,1024]{2,1,0:T(8,128)(2,1)} %get-tuple-element.68, s32[]{:T(128)S(6)} %copy.33, bf16[8,160,1024]{2,1,0:T(8,128)(2,1)} %get-tuple-element.71, s32[]{:T(128)} %bitcast.85, s32[]{:T(128)} %bitcast.86), kind=kLoop, calls=%fused_computation.clone.1 | loop fusion | bytes 525316 | tf_op jit(solution)/shard_map/vmap()/gather
  15.1 0.1 constant_dynamic-slice_fusion.2
  15.2 0.5 fusion.42
  15.7 2.9 %dynamic-slice_dynamic-update-slice_fusion.2 = bf16[8,128,1024]{2,1,0:T(8,128)(2,1)} fusion(bf16[8,128,1024]{2,1,0:T(8,128)(2,1)} %get-tuple-element.68, s32[]{:T(128)S(6)} %copy.33, bf16[8,160,1024]{2,1,0:T(8,128)(2,1)} %get-tuple-element.71, s32[]{:T(128)} %bitcast.85, s32[]{:T(128)} %bitcast.86), kind=kLoop, calls=%fused_computation.clone.1 | loop fusion | bytes 525316 | tf_op jit(solution)/shard_map/vmap()/gather
  18.6 0.1 constant_dynamic-slice_fusion.2
  18.7 0.5 fusion.42
  19.2 2.9 %dynamic-slice_dynamic-update-slice_fusion.2 = bf16[8,128,1024]{2,1,0:T(8,128)(2,1)} fusion(bf16[8,128,1024]{2,1,0:T(8,128)(2,1)} %get-tuple-element.68, s32[]{:T(128)S(6)} %copy.33, bf16[8,160,1024]{2,1,0:T(8,128)(2,1)} %get-tuple-element.71, s32[]{:T(128)} %bitcast.85, s32[]{:T(128)} %bitcast.86), kind=kLoop, calls=%fused_computation.clone.1 | loop fusion | bytes 525316 | tf_op jit(solution)/shard_map/vmap()/gather
  22.2 0.1 constant_dynamic-slice_fusion.2
  22.2 0.5 fusion.42
  22.8 2.9 %dynamic-slice_dynamic-update-slice_fusion.2 = bf16[8,128,1024]{2,1,0:T(8,128)(2,1)} fusion(bf16[8,128,1024]{2,1,0:T(8,128)(2,1)} %get-tuple-element.68, s32[]{:T(128)S(6)} %copy.33, bf16[8,160,1024]{2,1,0:T(8,128)(2,1)} %get-tuple-element.71, s32[]{:T(128)} %bitcast.85, s32[]{:T(128)} %bitcast.86), kind=kLoop, calls=%fused_computation.clone.1 | loop fusion | bytes 525316 | tf_op jit(solution)/shard_map/vmap()/gather
  25.7 0.1 constant_dynamic-slice_fusion.2
  25.8 0.5 fusion.42
  26.3 2.9 %dynamic-slice_dynamic-update-slice_fusion.2 = bf16[8,128,1024]{2,1,0:T(8,128)(2,1)} fusion(bf16[8,128,1024]{2,1,0:T(8,128)(2,1)} %get-tuple-element.68, s32[]{:T(128)S(6)} %copy.33, bf16[8,160,1024]{2,1,0:T(8,128)(2,1)} %get-tuple-element.71, s32[]{:T(128)} %bitcast.85, s32[]{:T(128)} %bitcast.86), kind=kLoop, calls=%fused_computation.clone.1 | loop fusion | bytes 525316 | tf_op jit(solution)/shard_map/vmap()/gather
  29.2 0.1 constant_dynamic-slice_fusion.2
  29.3 0.5 fusion.42
  29.8 2.9 %dynamic-slice_dynamic-update-slice_fusion.2 = bf16[8,128,1024]{2,1,0:T(8,128)(2,1)} fusion(bf16[8,128,1024]{2,1,0:T(8,128)(2,1)} %get-tuple-element.68, s32[]{:T(128)S(6)} %copy.33, bf16[8,160,1024]{2,1,0:T(8,128)(2,1)} %get-tuple-element.71, s32[]{:T(128)} %bitcast.85, s32[]{:T(128)} %bitcast.86), kind=kLoop, calls=%fused_computation.clone.1 | loop fusion | bytes 525316 | tf_op jit(solution)/shard_map/vmap()/gather
  32.8 0.1 constant_dynamic-slice_fusion.2
  32.8 0.5 fusion.42
  33.3 3.0 %dynamic-slice_dynamic-update-slice_fusion.2 = bf16[8,128,1024]{2,1,0:T(8,128)(2,1)} fusion(bf16[8,128,1024]{2,1,0:T(8,128)(2,1)} %get-tuple-element.68, s32[]{:T(128)S(6)} %copy.33, bf16[8,160,1024]{2,1,0:T(8,128)(2,1)} %get-tuple-element.71, s32[]{:T(128)} %bitcast.85, s32[]{:T(128)} %bitcast.86), kind=kLoop, calls=%fused_computation.clone.1 | loop fusion | bytes 525316 | tf_op jit(solution)/shard_map/vmap()/gather
  36.3 2.8 copy.20
  39.1 0.0 copy-done.5
  39.1 5.5 %convolution_convert_fusion = bf16[32,131072]{1,0:T(8,128)(2,1)} fusion(bf16[8,131072]{1,0:T(8,128)(2,1)S(1)} %bitcast.88, s32[8]{0:T(128)S(1)} %copy-done.5), kind=kOutput, calls=%fused_computation.2 | convolution fusion | flops 71303424 | bytes 10485792 | tf_op jit(solution)/shard_map/dot_general | solution.py:37
  44.6 0.0 all-reduce.6.cloned.1.call-update
  44.6 0.0 reduce-scatter.7.cloned.1.call-start
  45.3 0.0 copy-done.8
  45.3 0.6 dynamic-slice.4
  45.9 132.1 %all-reduce.6.cloned.1.call-done = bf16[32,131072]{1,0:T(8,128)(2,1)} async-done(((bf16[32,131072]{1,0:T(8,128)(2,1)}), bf16[32,131072]{1,0:T(8,128)(2,1)}) %all-reduce.6.cloned.1.call-update) | async-done | bytes 8388624
  178.1 3.8 %fusion.8 = f32[131072]{0:T(1024)S(1)} fusion(bf16[32,131072]{1,0:T(8,128)(2,1)} %all-reduce.6.cloned.1.call-done, u32[]{:T(128)} %bitcast.28), kind=kLoop, calls=%fused_computation.15 | loop fusion | flops 131072 | bytes 786436 | tf_op jit(solution)/shard_map/reshape | solution.py:44
  181.9 0.1 reshape.144
  182.0 0.0 copy-start.3
  182.0 0.0 copy-start.1
  182.0 0.8 fusion
  182.8 0.0 copy-start.4
  182.9 0.0 copy-start.6
  182.9 0.0 copy-start.7
  182.9 0.8 copy.15
  183.7 0.0 reduce-scatter.7.cloned.1.call-update
  183.8 24.8 %all_gather.3 = bf16[1,128,1024]{2,1,0:T(8,128)(2,1)S(1)} all-gather(bf16[1,128,128]{2,1,0:T(8,128)(2,1)S(1)} %copy-done.3), channel_id=1, replica_groups=mesh['dec'=32,'ch'=8] {'ch'}, dimensions={2}, use_global_device_ids=true | all-gather | bytes 294912 | tf_op jit(solution)/shard_map/all_gather | solution.py:59
  208.6 12.1 %reduce-scatter.7.cloned.1.call-done = bf16[128,128]{1,0:T(8,128)(2,1)} async-done(((bf16[1024,128]{1,0:T(8,128)(2,1)}), bf16[128,128]{1,0:T(8,128)(2,1)}) %reduce-scatter.7.cloned.1.call-update) | async-done | bytes 32784
  220.7 1.5 stack.2
  222.1 4.4 %all-to-all-start = ((bf16[8,128,128]{1,2,0:T(8,128)(2,1)}), bf16[8,128,128]{1,2,0:T(8,128)(2,1)S(1)}, u32[]{:S(2)}, u32[]{:S(2)}) async-start(bf16[8,128,128]{1,2,0:T(8,128)(2,1)} %stack.2), calls=%async_computation | async-start | bytes 524288 | tf_op jit(solution)/shard_map/all_to_all | solution.py:9
  226.6 0.0 reduce-scatter.9.cloned.1.call-start
  226.6 0.2 fusion.6
  226.9 0.0 copy-done.4
  226.9 0.1 fusion.33
  227.0 10.0 %all-to-all-done = bf16[8,128,128]{1,2,0:T(8,128)(2,1)S(1)} async-done(((bf16[8,128,128]{1,2,0:T(8,128)(2,1)}), bf16[8,128,128]{1,2,0:T(8,128)(2,1)S(1)}, u32[]{:S(2)}, u32[]{:S(2)}) %all-to-all-start) | async-done | bytes 262176 | tf_op jit(solution)/shard_map/all_to_all | solution.py:9
  237.1 0.0 copy-done.6
  237.1 1.2 fusion.4
  238.3 0.1 multiply_convert_fusion.3
  238.4 0.3 fusion.1
  238.8 0.8 copy.17
  239.6 0.0 reduce-scatter.9.cloned.1.call-update
  239.6 0.7 copy.16
  240.4 32.3 %reduce-scatter.9.cloned.1.call-done = bf16[128,128]{1,0:T(8,128)(2,1)} async-done(((bf16[1024,128]{1,0:T(8,128)(2,1)}), bf16[128,128]{1,0:T(8,128)(2,1)}) %reduce-scatter.9.cloned.1.call-update) | async-done | bytes 32784
  272.6 1.5 copy.18
  (15 shorter events, 0.1 us)
Async XLA Ops:
  7.2 174.8 %copy-start = (bf16[1024,1024]{1,0:T(8,128)(2,1)S(1)}, bf16[1024,1024]{1,0:T(8,128)(2,1)}, u32[]{:S(2)}) copy-start(bf16[1024,1024]{1,0:T(8,128)(2,1)} %param.21) | copy-start | bytes 6291460
  7.2 170.9 %all-reduce.6.cloned.1.call-start = ((), (), s32[]{:S(2)}) async-start(), calls=%async_computation.5 | async-start | bytes 16777216
  36.3 2.8 copy-start.5
  44.6 0.7 copy-start.8
  44.6 176.0 %reduce-scatter.7.cloned.1.call-start = ((), (), s32[]{:S(2)}) async-start(), calls=%async_computation.3 | async-start | bytes 294912
  182.0 1.8 copy-start.3
  182.0 44.6 %copy-start.1 = (bf16[1024,2,128]{2,1,0:T(2,128)(2,1)S(1)}, bf16[1024,2,128]{2,1,0:T(2,128)(2,1)}, u32[]{:S(2)}) copy-start(bf16[1024,2,128]{2,1,0:T(2,128)(2,1)} %param.16) | copy-start | bytes 1572868
  182.8 44.0 %copy-start.4 = (bf16[9,128]{1,0:T(8,128)(2,1)S(1)}, bf16[9,128]{1,0:T(8,128)(2,1)}, u32[]{:S(2)}) copy-start(bf16[9,128]{1,0:T(8,128)(2,1)} %param.17) | copy-start | bytes 6916
  182.9 54.2 %copy-start.6 = (f32[128]{0:T(128)S(1)}, f32[128]{0:T(128)}, u32[]{:S(2)}) copy-start(f32[128]{0:T(128)} %param.19) | copy-start | bytes 1540
  182.9 54.2 %copy-start.7 = (f32[128]{0:T(128)S(1)}, f32[128]{0:T(128)}, u32[]{:S(2)}) copy-start(f32[128]{0:T(128)} %param.18) | copy-start | bytes 1540
  222.1 14.9 %all-to-all-start = ((bf16[8,128,128]{1,2,0:T(8,128)(2,1)}), bf16[8,128,128]{1,2,0:T(8,128)(2,1)S(1)}, u32[]{:S(2)}, u32[]{:S(2)}) async-start(bf16[8,128,128]{1,2,0:T(8,128)(2,1)} %stack.2), calls=%async_computation | async-start | bytes 524288 | tf_op jit(solution)/shard_map/all_to_all | solution.py:9
  226.6 46.0 %reduce-scatter.9.cloned.1.call-start = ((), (), s32[]{:S(2)}) async-start(), calls=%async_computation.4 | async-start | bytes 294912
  226.9 12.7 %copy-start.2 = (bf16[128,128]{1,0:T(8,128)(2,1)S(1)}, bf16[128,128]{1,0:T(8,128)(2,1)}, u32[]{:S(2)}) copy-start(bf16[128,128]{1,0:T(8,128)(2,1)} %reduce-scatter.7.cloned.1.call-done) | copy-start | bytes 98308
Sparse Core Ops, SparseCore 0:
  44.8 133.2 all-reduce.5
  183.9 36.7 reduce-scatter.6
  239.7 32.8 reduce-scatter.8
